TPU v7x, 512 devices: a whole 4x4x16 slice. The times are simulated.
512 devices in a mesh: dp: 16 (over x, z_hi), row: 4 (over z_lo), col: 8 (over y, core).
Axes of the slice: x: 4, y: 4, z: 16 (z_hi: 4, z_lo: 4; z = z_hi * 4 + z_lo), core: 2. Of those that a mesh axis runs over, the one named last changes fastest.
Arguments:
- queries: bfloat16 [16, 48, 128, 1024], P('dp', 'row', 'col'), may hold values from -6 to 6
- keyvals: bfloat16 [16, 2, 48, 128, 1024], P('dp', None, 'row', 'col'), may hold values from -6 to 6
- out_weight: bfloat16 [16, 1024, 2048], P('dp', ('row', 'col')), may hold values from -0.75 to 0.75
- gate_weight: bfloat16 [16, 2048, 2048], P('dp', ('row', 'col')), may hold values from -0.125 to 0.125
- class_table: bfloat16 [16, 1000, 2048], P('dp', None, ('row', 'col')), may hold values from -5 to 5
- labels: int32 [16], P('dp'), may hold values from 0 to 999
- timesteps: int32 [16], P('dp'), may hold values from 0 to 999
- round_index: int32 [1], replicated, may hold values from 0 to 996
Outputs:
- update: bfloat16 [16, 48, 128, 2048], P('dp', 'row', 'col')
All inputs are finite; a program needn't handle non-finite values.
Results may differ from a plain program's by a relative error of at most 0.0081.
Values may be sent and summed in bfloat16 or wider, within the bound.
No kernel may reach another device: no remote copies, remote signals or barrier semaphores. Data moves between devices by JAX's collectives and lax.ppermute only.
A program may use at most 64 MiB of HBM per device.

v0:
```python
import functools
import math

import jax
import jax.numpy as jnp
from jax import lax
from jax.experimental import pallas as pl
from jax.experimental.pallas import tpu as pltpu
from jax.sharding import PartitionSpec as P

HDIM = 128
RADIUS = 3
F32 = jnp.float32
BF16 = jnp.bfloat16
GROUP = 4
EDGE = 4
PAD_ROWS = 2


def attend_kernel(q_ref, kv_ref, up_ref, down_ref, near_ref, far_ref, out_ref):
    rows, cols = 12, 16
    inner = q_ref.shape[1]
    row0 = lax.axis_index("row") * rows
    col_index = lax.axis_index("col")
    col0 = col_index * cols
    core = lax.rem(col_index, 2)
    near_base = jnp.where(core == 0, cols, -EDGE)
    far_base = jnp.where(core == 0, -EDGE, cols)
    queries = GROUP * cols
    band = (GROUP + 2 * RADIUS) * cols
    side = (GROUP + 2 * RADIUS + PAD_ROWS) * EDGE
    keys = band + 2 * side
    halo = RADIUS * cols
    factor = math.log2(math.e) / math.sqrt(HDIM)
    q_id = lax.broadcasted_iota(jnp.int32, (queries, keys), 0)
    k_id = lax.broadcasted_iota(jnp.int32, (queries, keys), 1)
    q_row, q_col = q_id // cols, q_id % cols
    side_id = jnp.where(k_id < band + side, k_id - band, k_id - band - side)
    k_row = jnp.where(k_id < band, k_id // cols, side_id // EDGE)
    base = jnp.where(k_id < band + side, near_base, far_base)
    k_col = jnp.where(k_id < band, k_id % cols, base + side_id % EDGE)
    d_row, d_col = k_row - q_row, k_col - q_col
    reach = (d_row >= 0) & (d_row <= 2 * RADIUS) & (d_col >= -RADIUS) & (d_col <= RADIUS)
    k_gcol = col0 + k_col
    reach = reach & (k_gcol >= 0) & (k_gcol < cols * lax.axis_size("col"))
    ones = jnp.ones((keys, HDIM), BF16)
    for group in range(rows // GROUP):
        k_grow = row0 + GROUP * group - RADIUS + k_row
        allowed = reach & (k_grow >= 0) & (k_grow < rows * lax.axis_size("row"))
        bias = jnp.where(allowed, F32(0.0), F32(-1e30))
        first = (GROUP * group - RADIUS) * cols
        last = first + band
        for head in range(inner // HDIM):
            lanes = slice(head * HDIM, (head + 1) * HDIM)

            def gathered(which):
                parts = []
                if first < 0:
                    parts.append(up_ref[which, halo + first : halo, lanes])
                parts.append(kv_ref[which, max(first, 0) : min(last, rows * cols), lanes])
                if last > rows * cols:
                    parts.append(down_ref[which, 0 : last - rows * cols, lanes])
                span = slice(GROUP * group * EDGE, GROUP * group * EDGE + side)
                parts.append(near_ref[which, span, lanes])
                parts.append(far_ref[which, span, lanes])
                return jnp.concatenate(parts, axis=0)

            q = q_ref[group * queries : (group + 1) * queries, lanes]
            scores = lax.dot_general(
                q, gathered(0), (((1,), (1,)), ((), ())), preferred_element_type=F32
            )
            scores = scores + bias
            top = jnp.max(scores, axis=-1, keepdims=True)
            weight = jnp.exp2((scores - top) * factor).astype(BF16)
            values = jnp.concatenate([gathered(1), ones], axis=1)
            both = jnp.dot(weight, values, preferred_element_type=F32)
            out_ref[group * queries : (group + 1) * queries, lanes] = (
                both[:, :HDIM] / both[:, HDIM:]
            ).astype(BF16)


def attend(q, kv, up, down, near, far):
    tokens, inner = q.shape
    return pl.pallas_call(
        attend_kernel,
        out_shape=jax.ShapeDtypeStruct((tokens, inner), BF16),
        in_specs=[pl.BlockSpec(memory_space=pltpu.VMEM)] * 6,
        out_specs=pl.BlockSpec(memory_space=pltpu.VMEM),
        compiler_params=pltpu.CompilerParams(vmem_limit_bytes=20 * 2**20),
        cost_estimate=pl.CostEstimate(flops=3000000000, bytes_accessed=0, transcendentals=0),
        name="attend",
    )(q, kv, up, down, near, far)


def in_vmem(count):
    return [pl.BlockSpec(memory_space=pltpu.VMEM)] * count


def picked_row(label, table_ref):
    columns, count = table_ref.shape
    kept = jnp.zeros((columns, 128), F32)
    for first in range(0, count, 128):
        width = min(128, count - first)
        block = table_ref[:, first : first + width].astype(F32)
        if width < 128:
            block = jnp.concatenate([block, jnp.zeros((columns, 128 - width), F32)], axis=1)
        ids = lax.broadcasted_iota(jnp.int32, (columns, 128), 1) + first
        kept = kept + jnp.where(ids.astype(F32) == label, block, F32(0.0))
    ones = jnp.ones((16, 128), BF16)
    return lax.dot_general(ones, kept.astype(BF16), (((1,), (1,)), ((), ())), preferred_element_type=F32)


def gate_product(row_a, row_b, embed, gate_weight):
    value = (0.5 * (row_a + row_b)).astype(BF16).astype(F32) + embed
    cond = (value / (1.0 + jnp.exp(-value))).astype(BF16)
    part = jnp.dot(cond, gate_weight, preferred_element_type=F32)
    return jnp.concatenate([part[:1, at * 128 : (at + 1) * 128] for at in range(16)], axis=0)


def to_block(value):
    high = value.astype(BF16).astype(F32)
    return jnp.concatenate([high, value - high], axis=0).astype(BF16)


def from_block(block):
    block = block.astype(F32)
    return block[:16] + block[16:]


FETCHES = 4


def begin_kernel(label_ref, step_ref, table_ref, gate_ref, ask_ref, table_out, gate_out, numbers, sems):
    label_copy = pltpu.make_async_copy(label_ref, numbers.at[0], sems.at[2 * FETCHES])
    step_copy = pltpu.make_async_copy(step_ref, numbers.at[1], sems.at[2 * FETCHES + 1])
    label_copy.start()
    step_copy.start()
    copies = []
    for kind, (source, target) in enumerate(((table_ref, table_out), (gate_ref, gate_out))):
        rows = source.shape[0] // FETCHES
        for part in range(FETCHES):
            span = pl.ds(part * rows, rows)
            copies.append(
                pltpu.make_async_copy(source.at[span, :], target.at[span, :], sems.at[kind * FETCHES + part])
            )
            copies[-1].start()
    shard_width, half_width = gate_ref.shape[0], gate_ref.shape[1] // 2
    first = (lax.axis_index("row") * lax.axis_size("col") + lax.axis_index("col")) * shard_width
    positions = lax.broadcasted_iota(jnp.int32, (1, shard_width), 1) + first
    freq_index = jnp.where(positions < half_width, positions, positions - half_width).astype(F32)
    frequency = jnp.exp(-math.log(10000.0) * freq_index / half_width)
    label_copy.wait()
    step_copy.wait()
    angle = jnp.full((1, 1), numbers[1, 0], jnp.int32).astype(F32) * frequency
    embed = jnp.where(positions < half_width, jnp.cos(angle), jnp.sin(angle))
    label = jnp.full((1, 1), numbers[0, 0], jnp.int32).astype(F32)
    for copy in copies[:FETCHES]:
        copy.wait()
    row = picked_row(label, table_out)[:1]
    ask_ref[:, 0:128] = jnp.concatenate([row, embed], axis=1)
    ask_ref[:, 128:256] = jnp.broadcast_to(label, (1, 128))
    for copy in copies[FETCHES:]:
        copy.wait()


def begin(label, step, table, gate_weight):
    return pl.pallas_call(
        begin_kernel,
        out_shape=(
            jax.ShapeDtypeStruct((1, 256), F32),
            jax.ShapeDtypeStruct(table.shape, BF16),
            jax.ShapeDtypeStruct(gate_weight.shape, BF16),
        ),
        in_specs=[pl.BlockSpec(memory_space=pltpu.HBM)] * 4,
        out_specs=tuple(in_vmem(3)),
        scratch_shapes=[pltpu.SMEM((2, 1), jnp.int32), pltpu.SemaphoreType.DMA((2 * FETCHES + 2,))],
        compiler_params=pltpu.CompilerParams(vmem_limit_bytes=56 * 2**20),
        name="begin",
    )(label, step, table, gate_weight)


def answer_kernel(asked_ref, table_ref, gate_ref, answer_ref):
    row = picked_row(asked_ref[:, 128:129], table_ref)
    part = gate_product(row, asked_ref[:, 0:64], asked_ref[:, 64:128], gate_ref[...])
    answer_ref[:, 0:128] = to_block(part)
    rows = jnp.concatenate([row, row], axis=1)
    answer_ref[:, 128:256] = jnp.concatenate([rows, rows], axis=0).astype(BF16)


def answer(asked, table, gate_weight):
    return pl.pallas_call(
        answer_kernel,
        out_shape=jax.ShapeDtypeStruct((32, 256), BF16),
        in_specs=in_vmem(3),
        out_specs=pl.BlockSpec(memory_space=pltpu.VMEM),
        compiler_params=pltpu.CompilerParams(vmem_limit_bytes=8 * 2**20),
        cost_estimate=pl.CostEstimate(flops=5000000000, bytes_accessed=0, transcendentals=0),
        name="answer",
    )(asked, table, gate_weight)


def mix_kernel(own_ref, peer_ref, ask_ref, answered_ref, gate_ref, sent_ref):
    shard, width = own_ref.shape
    peer = peer_ref[...].astype(F32)
    sent_ref[:, 0:width] = (0.5 * (own_ref[...].astype(F32) + peer)).astype(BF16)
    own_row = jnp.broadcast_to(ask_ref[:, 0:64], (16, 64))
    peer_row = answered_ref[0:16, 128:192].astype(F32)
    part = gate_product(own_row, peer_row, ask_ref[:, 64:128], gate_ref[...])
    part = 0.5 * (part + from_block(answered_ref[:, 0:128]))
    sent_ref[:, width : width + 128] = to_block(part)


def mix(own, peer, ask, answered, gate_weight):
    shard, width = own.shape
    return pl.pallas_call(
        mix_kernel,
        out_shape=jax.ShapeDtypeStruct((shard, width + 128), BF16),
        in_specs=in_vmem(5),
        out_specs=pl.BlockSpec(memory_space=pltpu.VMEM),
        compiler_params=pltpu.CompilerParams(vmem_limit_bytes=8 * 2**20),
        cost_estimate=pl.CostEstimate(flops=5000000000, bytes_accessed=0, transcendentals=0),
        name="mix",
    )(own, peer, ask, answered, gate_weight)


def stack_kernel(*refs):
    parts, out_ref = [refs[at] for at in (0, 3, 1, 2)], refs[4]
    shard = parts[0].shape[0]
    for index, part in enumerate(parts):
        out_ref[index * shard : (index + 1) * shard, :] = part[...]


def stacked(parts):
    rows, width = parts[0].shape
    return pl.pallas_call(
        stack_kernel,
        out_shape=jax.ShapeDtypeStruct((4 * rows, width), BF16),
        in_specs=in_vmem(4),
        out_specs=pl.BlockSpec(memory_space=pltpu.VMEM),
        compiler_params=pltpu.CompilerParams(vmem_limit_bytes=8 * 2**20),
        cost_estimate=pl.CostEstimate(flops=5000000000, bytes_accessed=0, transcendentals=0),
        name="stack",
    )(*parts)


def cut_kernel(kv_ref, after_ref, low_ref, high_ref, sems):
    tokens, halo = kv_ref.shape[1], low_ref.shape[1]
    lower = pltpu.make_async_copy(kv_ref.at[:, pl.ds(tokens - halo, halo), :], low_ref, sems.at[0])
    upper = pltpu.make_async_copy(kv_ref.at[:, pl.ds(0, halo), :], high_ref, sems.at[1])
    lower.start()
    upper.start()
    lower.wait()
    upper.wait()


def cut(kv, after):
    edge = jax.ShapeDtypeStruct((2, RADIUS * 16, kv.shape[2]), BF16)
    return pl.pallas_call(
        cut_kernel,
        out_shape=(edge, edge),
        in_specs=[pl.BlockSpec(memory_space=pl.ANY)] * 2,
        out_specs=tuple(in_vmem(2)),
        scratch_shapes=[pltpu.SemaphoreType.DMA((2,))],
        compiler_params=pltpu.CompilerParams(vmem_limit_bytes=8 * 2**20),
        name="cut",
    )(kv, after)


def edges_kernel(kv_ref, up_ref, down_ref, after_ref, near_ref, far_ref):
    cols = 16
    core = lax.rem(lax.axis_index("col"), 2)
    count = near_ref.shape[1]
    source = up_ref.shape[1] + kv_ref.shape[1] + down_ref.shape[1]
    out_id = lax.broadcasted_iota(jnp.int32, (count, source), 0)
    in_id = lax.broadcasted_iota(jnp.int32, (count, source), 1)
    right = (out_id // EDGE) * cols + cols - EDGE + out_id % EDGE
    left = (out_id // EDGE) * cols + out_id % EDGE
    right = jnp.where(in_id == right, F32(1.0), F32(0.0))
    left = jnp.where(in_id == left, F32(1.0), F32(0.0))
    first = core == 0
    pick_near = jnp.where(first, right, left).astype(BF16)
    pick_far = jnp.where(first, left, right).astype(BF16)
    for which in range(2):
        tall = jnp.concatenate([up_ref[which], kv_ref[which], down_ref[which]], axis=0)
        near_ref[which] = jnp.dot(pick_near, tall, preferred_element_type=F32).astype(BF16)
        far_ref[which] = jnp.dot(pick_far, tall, preferred_element_type=F32).astype(BF16)


def edges(kv, up, down, after):
    inner = kv.shape[2]
    count = (12 + 2 * RADIUS + PAD_ROWS) * EDGE
    edge = jax.ShapeDtypeStruct((2, count, inner), BF16)
    return pl.pallas_call(
        edges_kernel,
        out_shape=(edge, edge),
        in_specs=in_vmem(3) + [pl.BlockSpec(memory_space=pl.ANY)],
        out_specs=tuple(in_vmem(2)),
        compiler_params=pltpu.CompilerParams(vmem_limit_bytes=12 * 2**20),
        name="edges",
    )(kv, up, down, after)


def weight_rows(even, odd, at):
    rows = []
    for back in range(4):
        span = slice(back * 32, (back + 1) * 32)
        rows += [even[span, at], odd[span, at]]
    return rows


def gate_sum(pieces, width):
    total = jnp.zeros((32, 128), F32)
    for piece in pieces:
        for back in range(4):
            total = total + piece[back * 32 : (back + 1) * 32, width : width + 128].astype(F32)
    return total


def begin_project_kernel(a_ref, own, other, beside, own_x, other_x, beside_x, sum_ref, lanes_ref, gate_ref, held_ref):
    row, col = lax.axis_index("row"), lax.axis_index("col")
    core, place = lax.rem(col, 2), lax.div(col, 2)
    block = 256
    width = sum_ref.shape[1]
    odd_place, high_place = place & 1, place >= 2
    for back in range(4):
        start = pl.multiple_of((row ^ back) * block, block)
        lanes = a_ref[:, pl.ds(start, block)].astype(F32)
        first, second = lanes[:, :128], lanes[:, 128:]
        halves = jnp.where(high_place, second, first), jnp.where(high_place, first, second)
        halves = [pltpu.roll(half, 64 * odd_place, 1).astype(BF16) for half in halves]
        for slot, step in enumerate((0, 1, 3)):
            at = (step % 2) * 64
            held_ref[:, slot * block + back * 64 : slot * block + (back + 1) * 64] = halves[step // 2][:, at : at + 64]
        lanes_ref[:, back * 64 : (back + 1) * 64] = halves[1][:, :64]
    gate_ref[...] = gate_sum((own, beside, other, own_x, beside_x, other_x), width)
    part_width = 512

    def multiply(even, odd):
        for part in range(width // part_width):
            at = slice(part * part_width, (part + 1) * part_width)
            rows = []
            for even_piece, odd_piece in zip(even, odd):
                rows += weight_rows(even_piece, odd_piece, at)
            sum_ref[:, at] = jnp.dot(held_ref[...], jnp.concatenate(rows, axis=0), preferred_element_type=F32)

    @pl.when(core == 0)
    def _():
        multiply((own, beside, other), (own_x, beside_x, other_x))

    @pl.when(core == 1)
    def _():
        multiply((own_x, beside_x, other_x), (own, beside, other))


def begin_project(a, pieces):
    tokens, inner = a.shape
    width = pieces[0].shape[1] - 128
    return pl.pallas_call(
        begin_project_kernel,
        out_shape=(
            jax.ShapeDtypeStruct((tokens, width), F32),
            jax.ShapeDtypeStruct((tokens, inner // 4), BF16),
            jax.ShapeDtypeStruct((32, 128), F32),
        ),
        in_specs=in_vmem(7),
        out_specs=tuple(in_vmem(3)),
        scratch_shapes=[pltpu.VMEM((tokens, inner - inner // 4), BF16)],
        compiler_params=pltpu.CompilerParams(vmem_limit_bytes=20 * 2**20),
        name="begin_project",
    )(a, *pieces)


def project_kernel(sum_ref, lanes_ref, gate_ref, piece, piece_x, out_ref):
    core = lax.rem(lax.axis_index("col"), 2)
    width = out_ref.shape[1]
    total = gate_ref[...] + gate_sum((piece, piece_x), width)
    total = total[:16] + total[16:]
    gate = jnp.concatenate([total[at : at + 1] for at in range(16)], axis=1)
    part_width = 512

    def multiply(even, odd):
        for part in range(width // part_width):
            at = slice(part * part_width, (part + 1) * part_width)
            rows = jnp.concatenate(weight_rows(even, odd, at), axis=0)
            product = jnp.dot(lanes_ref[...], rows, preferred_element_type=F32) + sum_ref[:, at]
            out_ref[:, at] = (gate[:, at] * product).astype(BF16)

    @pl.when(core == 0)
    def _():
        multiply(piece, piece_x)

    @pl.when(core == 1)
    def _():
        multiply(piece_x, piece)


def project(begun, piece, piece_x):
    tokens, width = begun[0].shape
    return pl.pallas_call(
        project_kernel,
        out_shape=jax.ShapeDtypeStruct((tokens, width), BF16),
        in_specs=in_vmem(5),
        out_specs=pl.BlockSpec(memory_space=pltpu.VMEM),
        compiler_params=pltpu.CompilerParams(vmem_limit_bytes=16 * 2**20),
        name="project",
    )(*begun, piece, piece_x)


def local(queries, keyvals, out_weight, gate_weight, class_table, labels, timesteps, round_index):
    dp_count, row_count, col_count = (lax.axis_size(a) for a in ("dp", "row", "col"))
    bit_count = dp_count.bit_length() - 1
    tile_rows, tile_cols, inner = queries.shape[1:]
    up_pairs = [(i, i + 1) for i in range(row_count - 1)]
    down_pairs = [(j, i) for i, j in up_pairs]
    near_pairs = [(i, i ^ 1) for i in range(col_count)]
    far_pairs = [(i, i + 1) for i in range(1, col_count - 1, 2)]
    far_pairs = far_pairs + [(j, i) for i, j in far_pairs]

    def body(distance, ask, table, gate_weight, out_weight, q, kv):
        ahead = [(i, (i + distance) % dp_count) for i in range(dp_count)]
        behind = [(j, i) for i, j in ahead]
        asked = lax.ppermute(ask, "dp", behind)
        peer = lax.ppermute(out_weight, "dp", ahead)
        low, high = cut(kv, ask)
        up = lax.ppermute(low, "row", up_pairs)
        down = lax.ppermute(high, "row", down_pairs)
        answered = lax.ppermute(answer(asked, table, gate_weight), "dp", ahead)
        sent = mix(out_weight, peer, ask, answered, gate_weight)
        got = [sent] + [
            lax.ppermute(sent, "row", [(i, i ^ k) for i in range(row_count)]) for k in (2, 3, 1)
        ]
        stack = stacked(got)
        opposite, beside, other = (
            lax.ppermute(stack, "col", [(i, i ^ (2 * k)) for i in range(col_count)]) for k in (2, 1, 3)
        )
        near, far = edges(kv, up, down, sent)
        far = lax.ppermute(far, "col", far_pairs)
        near = lax.ppermute(near, "col", near_pairs)
        attended = attend(q, kv, up, down, near, far)
        mine, attended = lax.optimization_barrier((stack, attended))
        siblings = [lax.ppermute(part, "col", near_pairs) for part in (mine, opposite, other, beside)]
        mine_x, opposite_x, other_x, beside_x = siblings
        begun = begin_project(attended, (stack, other, beside, mine_x, other_x, beside_x))
        return project(begun, opposite, opposite_x)

    table = class_table[0].T
    ask, table, gate_weight = begin(labels, timesteps, table, gate_weight[0])
    result = lax.switch(
        round_index[0] % bit_count,
        [functools.partial(body, 2**bit) for bit in range(bit_count)],
        ask,
        table,
        gate_weight,
        out_weight[0],
        queries.reshape(-1, inner),
        keyvals.reshape(2, -1, inner),
    )
    return result.reshape(1, tile_rows, tile_cols, -1)


def solution(mesh):
    placed = (
        P("dp", "row", "col", None),
        P("dp", None, "row", "col", None),
        P("dp", ("row", "col"), None),
        P("dp", ("row", "col"), None),
        P("dp", None, ("row", "col")),
        P("dp"),
        P("dp"),
        P(),
    )
    return jax.shard_map(
        local, mesh=mesh, in_specs=placed, out_specs=P("dp", "row", "col", None), check_vma=False
    )
```

profile of v0, /device:TPU:293, one launch (start us, length us, event | category | flops | bytes accessed | tf_op | source)
XLA Modules:
  0.0 77.8 jit_solution(11661649798648125449)
XLA Ops:
  2.0 1.1 %begin.1 = (f32[1,256]{1,0:T(1,128)S(1)}, bf16[64,1000]{1,0:T(8,128)(2,1)S(1)}, bf16[64,2048]{1,0:T(8,128)(2,1)S(1)}) custom-call(s32[1]{0:T(128)S(6)} %copy.17.label_ref, s32[1]{0:T(128)S(6)} %copy.18.step_ref, bf16[64,1000]{1,0:T(8,128)(2,1)} %bitcast.24, bf16[64,2048]{1,0:T(8,128)(2,1)} %bitcast.23), custom_call_target="tpu_custom_call" | custom-call | tf_op jit(solution)/shard_map/begin/pallas_call | solution.py:167
  3.1 73.8 %conditional.1 = (bf16[1,12,16,2048]{3,2,1,0:T(8,128)(2,1)S(1)}) conditional(s32[]{:T(128)} %clamp.3, (bf16[32,2048]{1,0:T(8,128)(2,1)}, f32[1,256]{1,0:T(1,128)S(1)}, bf16[64,1000]{1,0:T(8,128)(2,1)S(1)}, bf16[64,2048]{1,0:T(8,128)(2,1)S(1)}, bf16[2,192,1024]{2,1,0:T(8,128)(2,1)}, ...), branch_computations={%region_0.1_spmd, %region_1.2_spmd, %region_2.3_spmd, %region_3.4_... | conditional | flops 17999998976 | bytes 27300612 | solution.py:448
  3.1 2.2 %collective-permute-start.35 = (f32[1,256]{1,0:T(1,128)S(1)}, f32[1,256]{1,0:T(1,128)S(1)}, u32[]{:S(2)}, u32[]{:S(2)}) collective-permute-start(f32[1,256]{1,0:T(1,128)S(1)} %get-tuple-element.90.ask_ref.after_ref), channel_id=1, source_target_pairs={{128,0},{160,32},{192,64},{224,96},{256,128},{288,160},{320,192},{... | collective-permute-start | bytes 3080 | tf_op jit(solution)/shard_map/cond/branch_2_fun/ppermute | solution.py:422
  5.3 3.1 %collective-permute-start.34 = (bf16[32,2048]{1,0:T(8,128)(2,1)}, bf16[32,2048]{1,0:T(8,128)(2,1)S(1)}, u32[]{:S(2)}, u32[]{:S(2)}) collective-permute-start(bf16[32,2048]{1,0:T(8,128)(2,1)} %get-tuple-element.89.own_ref), channel_id=1, source_target_pairs={{0,128},{32,160},{64,192},{96,224},{128,256},{160,288},{192,320},{... | collective-permute-start | bytes 393224 | tf_op jit(solution)/shard_map/cond/branch_2_fun/ppermute | solution.py:423
  8.4 0.0 collective-permute-done.35.asked_ref
  8.4 0.0 copy-start.2
  8.4 0.0 copy-start.11
  8.4 0.4 answer.6
  8.8 4.0 %collective-permute-start.36 = (bf16[32,256]{1,0:T(8,128)(2,1)S(1)}, bf16[32,256]{1,0:T(8,128)(2,1)S(1)}, u32[]{:S(2)}, u32[]{:S(2)}) collective-permute-start(bf16[32,256]{1,0:T(8,128)(2,1)S(1)} %answer.6), channel_id=1, source_target_pairs={{0,128},{32,160},{64,192},{96,224},{128,256},{160,288},{192,320},{... | collective-permute-start | bytes 49160 | tf_op jit(solution)/shard_map/cond/branch_2_fun/ppermute | solution.py:427
  12.9 0.3 cut.6
  13.2 2.8 %collective-permute-start.40 = (bf16[2,48,1024]{2,1,0:T(8,128)(2,1)S(1)}, bf16[2,48,1024]{2,1,0:T(8,128)(2,1)S(1)}, u32[]{:S(2)}, u32[]{:S(2)}) collective-permute-start(bf16[2,48,1024]{2,1,0:T(8,128)(2,1)S(1)} %get-tuple-element.95), channel_id=1, source_target_pairs={{0,8},{8,16},{16,24},{1,9},{9,17},{17,25},{2,10},{10,18},{18,26},{... | collective-permute-start | bytes 589832 | tf_op jit(solution)/shard_map/cond/branch_2_fun/ppermute | solution.py:425
  16.0 2.6 %collective-permute-start.41 = (bf16[2,48,1024]{2,1,0:T(8,128)(2,1)S(1)}, bf16[2,48,1024]{2,1,0:T(8,128)(2,1)S(1)}, u32[]{:S(2)}, u32[]{:S(2)}) collective-permute-start(bf16[2,48,1024]{2,1,0:T(8,128)(2,1)S(1)} %get-tuple-element.96), channel_id=1, source_target_pairs={{8,0},{16,8},{24,16},{9,1},{17,9},{25,17},{10,2},{18,10},{26,18},{... | collective-permute-start | bytes 589832 | tf_op jit(solution)/shard_map/cond/branch_2_fun/ppermute | solution.py:426
  18.6 0.0 collective-permute-done.36.answered_ref
  18.7 0.0 collective-permute-done.34.peer_ref
  18.7 0.2 mix.6.refs_0_.after_ref
  18.9 3.1 %collective-permute-start.37 = (bf16[32,2176]{1,0:T(8,128)(2,1)S(1)}, bf16[32,2176]{1,0:T(8,128)(2,1)S(1)}, u32[]{:S(2)}, u32[]{:S(2)}) collective-permute-start(bf16[32,2176]{1,0:T(8,128)(2,1)S(1)} %mix.6.refs_0_.after_ref), channel_id=1, source_target_pairs={{0,16},{8,24},{16,0},{24,8},{1,17},{9,25},{17,1},{25,9},{2,18},{10... | collective-permute-start | bytes 417800 | tf_op jit(solution)/shard_map/cond/branch_2_fun/ppermute | solution.py:430
  22.0 1.9 %collective-permute-start.38 = (bf16[32,2176]{1,0:T(8,128)(2,1)S(1)}, bf16[32,2176]{1,0:T(8,128)(2,1)S(1)}, u32[]{:S(2)}, u32[]{:S(2)}) collective-permute-start(bf16[32,2176]{1,0:T(8,128)(2,1)S(1)} %mix.6.refs_0_.after_ref), channel_id=1, source_target_pairs={{0,24},{8,16},{16,8},{24,0},{1,25},{9,17},{17,9},{25,1},{2,26},{10... | collective-permute-start | bytes 417800 | tf_op jit(solution)/shard_map/cond/branch_2_fun/ppermute | solution.py:430
  24.0 4.2 %collective-permute-start.39 = (bf16[32,2176]{1,0:T(8,128)(2,1)S(1)}, bf16[32,2176]{1,0:T(8,128)(2,1)S(1)}, u32[]{:S(2)}, u32[]{:S(2)}) collective-permute-start(bf16[32,2176]{1,0:T(8,128)(2,1)S(1)} %mix.6.refs_0_.after_ref), channel_id=1, source_target_pairs={{0,8},{8,0},{16,24},{24,16},{1,9},{9,1},{17,25},{25,17},{2,10},{10... | collective-permute-start | bytes 417800 | tf_op jit(solution)/shard_map/cond/branch_2_fun/ppermute | solution.py:430
  28.2 0.0 collective-permute-done.40.up_ref
  28.2 0.0 collective-permute-done.41.down_ref
  28.2 0.7 edges.6
  28.9 7.1 %collective-permute-start.42 = (bf16[2,80,1024]{2,1,0:T(8,128)(2,1)S(1)}, bf16[2,80,1024]{2,1,0:T(8,128)(2,1)S(1)}, u32[]{:S(2)}, u32[]{:S(2)}) collective-permute-start(bf16[2,80,1024]{2,1,0:T(8,128)(2,1)S(1)} %get-tuple-element.97), channel_id=1, source_target_pairs={{0,1},{1,0},{2,3},{3,2},{4,5},{5,4},{6,7},{7,6},{8,9},{9,8},{10,11... | collective-permute-start | bytes 983048 | tf_op jit(solution)/shard_map/cond/branch_2_fun/ppermute | solution.py:438
  36.0 0.0 copy-start.7
  36.1 3.2 %collective-permute-start.43 = (bf16[2,80,1024]{2,1,0:T(8,128)(2,1)S(1)}, bf16[2,80,1024]{2,1,0:T(8,128)(2,1)S(1)}, u32[]{:S(2)}, u32[]{:S(2)}) collective-permute-start(bf16[2,80,1024]{2,1,0:T(8,128)(2,1)S(1)} %get-tuple-element.98), channel_id=1, source_target_pairs={{1,2},{3,4},{5,6},{2,1},{4,3},{6,5},{9,10},{11,12},{13,14},{10,9},... | collective-permute-start | bytes 983048 | tf_op jit(solution)/shard_map/cond/branch_2_fun/ppermute | solution.py:437
  39.3 0.0 collective-permute-done.37.refs_1_
  39.3 0.0 collective-permute-done.38.refs_2_
  39.3 0.0 collective-permute-done.39.refs_3_
  39.4 2.2 %collective-permute-start.44 = (bf16[128,2176]{1,0:T(8,128)(2,1)S(1)}, bf16[128,2176]{1,0:T(8,128)(2,1)S(1)}, u32[]{:S(2)}, u32[]{:S(2)}) collective-permute-start(bf16[128,2176]{1,0:T(8,128)(2,1)S(1)} %stack.6.own), channel_id=1, source_target_pairs={{0,6},{1,7},{2,4},{3,5},{4,2},{5,3},{6,0},{7,1},{8,14},{9,15},{10,... | collective-permute-start | bytes 1671176 | tf_op jit(solution)/shard_map/cond/branch_2_fun/ppermute | solution.py:434
  41.6 3.9 %collective-permute-start.45 = (bf16[128,2176]{1,0:T(8,128)(2,1)S(1)}, bf16[128,2176]{1,0:T(8,128)(2,1)S(1)}, u32[]{:S(2)}, u32[]{:S(2)}) collective-permute-start(bf16[128,2176]{1,0:T(8,128)(2,1)S(1)} %stack.6.own), channel_id=1, source_target_pairs={{0,2},{1,3},{2,0},{3,1},{4,6},{5,7},{6,4},{7,5},{8,10},{9,11},{10,... | collective-permute-start | bytes 1671176 | tf_op jit(solution)/shard_map/cond/branch_2_fun/ppermute | solution.py:434
  45.5 3.5 %collective-permute-start.49 = (bf16[128,2176]{1,0:T(8,128)(2,1)S(1)}, bf16[128,2176]{1,0:T(8,128)(2,1)S(1)}, u32[]{:S(2)}, u32[]{:S(2)}) collective-permute-start(bf16[128,2176]{1,0:T(8,128)(2,1)S(1)} %stack.6.own), channel_id=1, source_target_pairs={{0,4},{1,5},{2,6},{3,7},{4,0},{5,1},{6,2},{7,3},{8,12},{9,13},{10,... | collective-permute-start | bytes 1671176 | tf_op jit(solution)/shard_map/cond/branch_2_fun/ppermute | solution.py:434
  49.0 0.0 collective-permute-done.42.near_ref
  49.0 0.0 collective-permute-done.43.far_ref
  49.0 1.4 %attend.6.a_ref = bf16[192,1024]{1,0:T(8,128)(2,1)S(1)} custom-call(bf16[192,1024]{1,0:T(8,128)(2,1)S(1)} %copy-done.7, bf16[2,192,1024]{2,1,0:T(8,128)(2,1)S(1)} %copy-done.2, bf16[2,48,1024]{2,1,0:T(8,128)(2,1)S(1)} %collective-permute-done.40.up_ref, bf16[2,48,1024]{2,1,0:T(8,128)(2,1)S(1)} %collective-permute-done.41.down_ref, ...), custom_call_target="tpu_custom_call" | custom-call | flops 3000000000 | tf_op jit(solution)/shard_map/cond/branch_2_fun/attend/pallas_call | solution.py:84
  50.4 2.2 %collective-permute-start.46 = (bf16[128,2176]{1,0:T(8,128)(2,1)S(1)}, bf16[128,2176]{1,0:T(8,128)(2,1)S(1)}, u32[]{:S(2)}, u32[]{:S(2)}) collective-permute-start(bf16[128,2176]{1,0:T(8,128)(2,1)S(1)} %stack.6.own), channel_id=1, source_target_pairs={{0,1},{1,0},{2,3},{3,2},{4,5},{5,4},{6,7},{7,6},{8,9},{9,8},{10,11... | collective-permute-start | bytes 1671176 | tf_op jit(solution)/shard_map/cond/branch_2_fun/ppermute | solution.py:441
  52.6 4.3 %collective-permute-done.44.other = bf16[128,2176]{1,0:T(8,128)(2,1)S(1)} collective-permute-done((bf16[128,2176]{1,0:T(8,128)(2,1)S(1)}, bf16[128,2176]{1,0:T(8,128)(2,1)S(1)}, u32[]{:S(2)}, u32[]{:S(2)}) %collective-permute-start.44) | collective-permute-done | bytes 557088 | tf_op jit(solution)/shard_map/cond/branch_2_fun/ppermute | solution.py:434
  57.0 2.3 %collective-permute-start.47 = (bf16[128,2176]{1,0:T(8,128)(2,1)S(1)}, bf16[128,2176]{1,0:T(8,128)(2,1)S(1)}, u32[]{:S(2)}, u32[]{:S(2)}) collective-permute-start(bf16[128,2176]{1,0:T(8,128)(2,1)S(1)} %collective-permute-done.44.other), channel_id=1, source_target_pairs={{0,1},{1,0},{2,3},{3,2},{4,5},{5,4},{6,7},{7,6},{8,9},{9,8},{10,11... | collective-permute-start | bytes 1671176 | tf_op jit(solution)/shard_map/cond/branch_2_fun/ppermute | solution.py:441
  59.3 0.0 collective-permute-done.45.beside
  59.3 4.1 %collective-permute-start.48 = (bf16[128,2176]{1,0:T(8,128)(2,1)S(1)}, bf16[128,2176]{1,0:T(8,128)(2,1)S(1)}, u32[]{:S(2)}, u32[]{:S(2)}) collective-permute-start(bf16[128,2176]{1,0:T(8,128)(2,1)S(1)} %collective-permute-done.45.beside), channel_id=1, source_target_pairs={{0,1},{1,0},{2,3},{3,2},{4,5},{5,4},{6,7},{7,6},{8,9},{9,8},{10,11... | collective-permute-start | bytes 1671176 | tf_op jit(solution)/shard_map/cond/branch_2_fun/ppermute | solution.py:441
  63.3 8.6 %collective-permute-done.49.piece = bf16[128,2176]{1,0:T(8,128)(2,1)S(1)} collective-permute-done((bf16[128,2176]{1,0:T(8,128)(2,1)S(1)}, bf16[128,2176]{1,0:T(8,128)(2,1)S(1)}, u32[]{:S(2)}, u32[]{:S(2)}) %collective-permute-start.49) | collective-permute-done | bytes 557088 | tf_op jit(solution)/shard_map/cond/branch_2_fun/ppermute | solution.py:434
  72.0 2.5 %collective-permute-start.50 = (bf16[128,2176]{1,0:T(8,128)(2,1)S(1)}, bf16[128,2176]{1,0:T(8,128)(2,1)S(1)}, u32[]{:S(2)}, u32[]{:S(2)}) collective-permute-start(bf16[128,2176]{1,0:T(8,128)(2,1)S(1)} %collective-permute-done.49.piece), channel_id=1, source_target_pairs={{0,1},{1,0},{2,3},{3,2},{4,5},{5,4},{6,7},{7,6},{8,9},{9,8},{10,11... | collective-permute-start | bytes 1671176 | tf_op jit(solution)/shard_map/cond/branch_2_fun/ppermute | solution.py:441
  74.5 0.0 collective-permute-done.46.own_x
  74.5 0.0 collective-permute-done.47.other_x
  74.5 0.0 collective-permute-done.48.beside_x
  74.5 1.3 %begin_project.6 = (f32[192,2048]{1,0:T(8,128)S(1)}, bf16[192,256]{1,0:T(8,128)(2,1)S(1)}, f32[32,128]{1,0:T(8,128)S(1)}) custom-call(bf16[192,1024]{1,0:T(8,128)(2,1)S(1)} %attend.6.a_ref, bf16[128,2176]{1,0:T(8,128)(2,1)S(1)} %stack.6.own, bf16[128,2176]{1,0:T(8,128)(2,1)S(1)} %collective-permute-done.44.other, ...), custom_call_target="tpu_custom_call" | custom-call | tf_op jit(solution)/shard_map/cond/branch_2_fun/begin_project/pallas_call | solution.py:358
  75.8 0.2 collective-permute-done.50.piece_x
  76.0 0.4 project.6
  76.9 0.0 copy-start.4
  76.9 0.9 %copy-done.4 = bf16[1,12,16,2048]{3,2,1,0:T(8,128)(2,1)} copy-done((bf16[1,12,16,2048]{3,2,1,0:T(8,128)(2,1)}, bf16[1,12,16,2048]{3,2,1,0:T(8,128)(2,1)S(1)}, u32[]{:S(2)}) %copy-start.4) | copy-done | bytes 786456
  (4 shorter events, 0.0 us)
Async XLA Ops:
  3.1 5.3 %collective-permute-start.35 = (f32[1,256]{1,0:T(1,128)S(1)}, f32[1,256]{1,0:T(1,128)S(1)}, u32[]{:S(2)}, u32[]{:S(2)}) collective-permute-start(f32[1,256]{1,0:T(1,128)S(1)} %get-tuple-element.90.ask_ref.after_ref), channel_id=1, source_target_pairs={{128,0},{160,32},{192,64},{224,96},{256,128},{288,160},{320,192},{... | collective-permute-start | bytes 3080 | tf_op jit(solution)/shard_map/cond/branch_2_fun/ppermute | solution.py:422
  5.3 13.4 %collective-permute-start.34 = (bf16[32,2048]{1,0:T(8,128)(2,1)}, bf16[32,2048]{1,0:T(8,128)(2,1)S(1)}, u32[]{:S(2)}, u32[]{:S(2)}) collective-permute-start(bf16[32,2048]{1,0:T(8,128)(2,1)} %get-tuple-element.89.own_ref), channel_id=1, source_target_pairs={{0,128},{32,160},{64,192},{96,224},{128,256},{160,288},{192,320},{... | collective-permute-start | bytes 393224 | tf_op jit(solution)/shard_map/cond/branch_2_fun/ppermute | solution.py:423
  8.4 4.5 %copy-start.2 = (bf16[2,192,1024]{2,1,0:T(8,128)(2,1)S(1)}, bf16[2,192,1024]{2,1,0:T(8,128)(2,1)}, u32[]{:S(2)}) copy-start(bf16[2,192,1024]{2,1,0:T(8,128)(2,1)} %get-tuple-element.94.kv_ref) | copy-start | bytes 2359300 | tf_op jit(solution)/shard_map/cond
  8.4 10.3 %copy-start.11 = (bf16[32,2048]{1,0:T(8,128)(2,1)S(1)}, bf16[32,2048]{1,0:T(8,128)(2,1)}, u32[]{:S(2)}) copy-start(bf16[32,2048]{1,0:T(8,128)(2,1)} %get-tuple-element.89.own_ref) | copy-start | bytes 393220 | tf_op jit(solution)/shard_map/cond
  8.8 9.8 %collective-permute-start.36 = (bf16[32,256]{1,0:T(8,128)(2,1)S(1)}, bf16[32,256]{1,0:T(8,128)(2,1)S(1)}, u32[]{:S(2)}, u32[]{:S(2)}) collective-permute-start(bf16[32,256]{1,0:T(8,128)(2,1)S(1)} %answer.6), channel_id=1, source_target_pairs={{0,128},{32,160},{64,192},{96,224},{128,256},{160,288},{192,320},{... | collective-permute-start | bytes 49160 | tf_op jit(solution)/shard_map/cond/branch_2_fun/ppermute | solution.py:427
  13.2 15.1 %collective-permute-start.40 = (bf16[2,48,1024]{2,1,0:T(8,128)(2,1)S(1)}, bf16[2,48,1024]{2,1,0:T(8,128)(2,1)S(1)}, u32[]{:S(2)}, u32[]{:S(2)}) collective-permute-start(bf16[2,48,1024]{2,1,0:T(8,128)(2,1)S(1)} %get-tuple-element.95), channel_id=1, source_target_pairs={{0,8},{8,16},{16,24},{1,9},{9,17},{17,25},{2,10},{10,18},{18,26},{... | collective-permute-start | bytes 589832 | tf_op jit(solution)/shard_map/cond/branch_2_fun/ppermute | solution.py:425
  16.0 12.2 %collective-permute-start.41 = (bf16[2,48,1024]{2,1,0:T(8,128)(2,1)S(1)}, bf16[2,48,1024]{2,1,0:T(8,128)(2,1)S(1)}, u32[]{:S(2)}, u32[]{:S(2)}) collective-permute-start(bf16[2,48,1024]{2,1,0:T(8,128)(2,1)S(1)} %get-tuple-element.96), channel_id=1, source_target_pairs={{8,0},{16,8},{24,16},{9,1},{17,9},{25,17},{10,2},{18,10},{26,18},{... | collective-permute-start | bytes 589832 | tf_op jit(solution)/shard_map/cond/branch_2_fun/ppermute | solution.py:426
  18.9 20.4 %collective-permute-start.37 = (bf16[32,2176]{1,0:T(8,128)(2,1)S(1)}, bf16[32,2176]{1,0:T(8,128)(2,1)S(1)}, u32[]{:S(2)}, u32[]{:S(2)}) collective-permute-start(bf16[32,2176]{1,0:T(8,128)(2,1)S(1)} %mix.6.refs_0_.after_ref), channel_id=1, source_target_pairs={{0,16},{8,24},{16,0},{24,8},{1,17},{9,25},{17,1},{25,9},{2,18},{10... | collective-permute-start | bytes 417800 | tf_op jit(solution)/shard_map/cond/branch_2_fun/ppermute | solution.py:430
  22.0 17.3 %collective-permute-start.38 = (bf16[32,2176]{1,0:T(8,128)(2,1)S(1)}, bf16[32,2176]{1,0:T(8,128)(2,1)S(1)}, u32[]{:S(2)}, u32[]{:S(2)}) collective-permute-start(bf16[32,2176]{1,0:T(8,128)(2,1)S(1)} %mix.6.refs_0_.after_ref), channel_id=1, source_target_pairs={{0,24},{8,16},{16,8},{24,0},{1,25},{9,17},{17,9},{25,1},{2,26},{10... | collective-permute-start | bytes 417800 | tf_op jit(solution)/shard_map/cond/branch_2_fun/ppermute | solution.py:430
  24.0 15.4 %collective-permute-start.39 = (bf16[32,2176]{1,0:T(8,128)(2,1)S(1)}, bf16[32,2176]{1,0:T(8,128)(2,1)S(1)}, u32[]{:S(2)}, u32[]{:S(2)}) collective-permute-start(bf16[32,2176]{1,0:T(8,128)(2,1)S(1)} %mix.6.refs_0_.after_ref), channel_id=1, source_target_pairs={{0,8},{8,0},{16,24},{24,16},{1,9},{9,1},{17,25},{25,17},{2,10},{10... | collective-permute-start | bytes 417800 | tf_op jit(solution)/shard_map/cond/branch_2_fun/ppermute | solution.py:430
  28.9 20.1 %collective-permute-start.42 = (bf16[2,80,1024]{2,1,0:T(8,128)(2,1)S(1)}, bf16[2,80,1024]{2,1,0:T(8,128)(2,1)S(1)}, u32[]{:S(2)}, u32[]{:S(2)}) collective-permute-start(bf16[2,80,1024]{2,1,0:T(8,128)(2,1)S(1)} %get-tuple-element.97), channel_id=1, source_target_pairs={{0,1},{1,0},{2,3},{3,2},{4,5},{5,4},{6,7},{7,6},{8,9},{9,8},{10,11... | collective-permute-start | bytes 983048 | tf_op jit(solution)/shard_map/cond/branch_2_fun/ppermute | solution.py:438
  36.0 13.0 %copy-start.7 = (bf16[192,1024]{1,0:T(8,128)(2,1)S(1)}, bf16[192,1024]{1,0:T(8,128)(2,1)}, u32[]{:S(2)}) copy-start(bf16[192,1024]{1,0:T(8,128)(2,1)} %get-tuple-element.93.q_ref) | copy-start | bytes 1179652 | tf_op jit(solution)/shard_map/cond
  36.1 13.0 %collective-permute-start.43 = (bf16[2,80,1024]{2,1,0:T(8,128)(2,1)S(1)}, bf16[2,80,1024]{2,1,0:T(8,128)(2,1)S(1)}, u32[]{:S(2)}, u32[]{:S(2)}) collective-permute-start(bf16[2,80,1024]{2,1,0:T(8,128)(2,1)S(1)} %get-tuple-element.98), channel_id=1, source_target_pairs={{1,2},{3,4},{5,6},{2,1},{4,3},{6,5},{9,10},{11,12},{13,14},{10,9},... | collective-permute-start | bytes 983048 | tf_op jit(solution)/shard_map/cond/branch_2_fun/ppermute | solution.py:437
  39.4 17.6 %collective-permute-start.44 = (bf16[128,2176]{1,0:T(8,128)(2,1)S(1)}, bf16[128,2176]{1,0:T(8,128)(2,1)S(1)}, u32[]{:S(2)}, u32[]{:S(2)}) collective-permute-start(bf16[128,2176]{1,0:T(8,128)(2,1)S(1)} %stack.6.own), channel_id=1, source_target_pairs={{0,6},{1,7},{2,4},{3,5},{4,2},{5,3},{6,0},{7,1},{8,14},{9,15},{10,... | collective-permute-start | bytes 1671176 | tf_op jit(solution)/shard_map/cond/branch_2_fun/ppermute | solution.py:434
  41.6 17.6 %collective-permute-start.45 = (bf16[128,2176]{1,0:T(8,128)(2,1)S(1)}, bf16[128,2176]{1,0:T(8,128)(2,1)S(1)}, u32[]{:S(2)}, u32[]{:S(2)}) collective-permute-start(bf16[128,2176]{1,0:T(8,128)(2,1)S(1)} %stack.6.own), channel_id=1, source_target_pairs={{0,2},{1,3},{2,0},{3,1},{4,6},{5,7},{6,4},{7,5},{8,10},{9,11},{10,... | collective-permute-start | bytes 1671176 | tf_op jit(solution)/shard_map/cond/branch_2_fun/ppermute | solution.py:434
  45.5 26.5 %collective-permute-start.49 = (bf16[128,2176]{1,0:T(8,128)(2,1)S(1)}, bf16[128,2176]{1,0:T(8,128)(2,1)S(1)}, u32[]{:S(2)}, u32[]{:S(2)}) collective-permute-start(bf16[128,2176]{1,0:T(8,128)(2,1)S(1)} %stack.6.own), channel_id=1, source_target_pairs={{0,4},{1,5},{2,6},{3,7},{4,0},{5,1},{6,2},{7,3},{8,12},{9,13},{10,... | collective-permute-start | bytes 1671176 | tf_op jit(solution)/shard_map/cond/branch_2_fun/ppermute | solution.py:434
  50.4 24.0 %collective-permute-start.46 = (bf16[128,2176]{1,0:T(8,128)(2,1)S(1)}, bf16[128,2176]{1,0:T(8,128)(2,1)S(1)}, u32[]{:S(2)}, u32[]{:S(2)}) collective-permute-start(bf16[128,2176]{1,0:T(8,128)(2,1)S(1)} %stack.6.own), channel_id=1, source_target_pairs={{0,1},{1,0},{2,3},{3,2},{4,5},{5,4},{6,7},{7,6},{8,9},{9,8},{10,11... | collective-permute-start | bytes 1671176 | tf_op jit(solution)/shard_map/cond/branch_2_fun/ppermute | solution.py:441
  57.0 17.5 %collective-permute-start.47 = (bf16[128,2176]{1,0:T(8,128)(2,1)S(1)}, bf16[128,2176]{1,0:T(8,128)(2,1)S(1)}, u32[]{:S(2)}, u32[]{:S(2)}) collective-permute-start(bf16[128,2176]{1,0:T(8,128)(2,1)S(1)} %collective-permute-done.44.other), channel_id=1, source_target_pairs={{0,1},{1,0},{2,3},{3,2},{4,5},{5,4},{6,7},{7,6},{8,9},{9,8},{10,11... | collective-permute-start | bytes 1671176 | tf_op jit(solution)/shard_map/cond/branch_2_fun/ppermute | solution.py:441
  59.3 15.2 %collective-permute-start.48 = (bf16[128,2176]{1,0:T(8,128)(2,1)S(1)}, bf16[128,2176]{1,0:T(8,128)(2,1)S(1)}, u32[]{:S(2)}, u32[]{:S(2)}) collective-permute-start(bf16[128,2176]{1,0:T(8,128)(2,1)S(1)} %collective-permute-done.45.beside), channel_id=1, source_target_pairs={{0,1},{1,0},{2,3},{3,2},{4,5},{5,4},{6,7},{7,6},{8,9},{9,8},{10,11... | collective-permute-start | bytes 1671176 | tf_op jit(solution)/shard_map/cond/branch_2_fun/ppermute | solution.py:441
  72.0 4.1 %collective-permute-start.50 = (bf16[128,2176]{1,0:T(8,128)(2,1)S(1)}, bf16[128,2176]{1,0:T(8,128)(2,1)S(1)}, u32[]{:S(2)}, u32[]{:S(2)}) collective-permute-start(bf16[128,2176]{1,0:T(8,128)(2,1)S(1)} %collective-permute-done.49.piece), channel_id=1, source_target_pairs={{0,1},{1,0},{2,3},{3,2},{4,5},{5,4},{6,7},{7,6},{8,9},{9,8},{10,11... | collective-permute-start | bytes 1671176 | tf_op jit(solution)/shard_map/cond/branch_2_fun/ppermute | solution.py:441
  76.9 0.9 %copy-start.4 = (bf16[1,12,16,2048]{3,2,1,0:T(8,128)(2,1)}, bf16[1,12,16,2048]{3,2,1,0:T(8,128)(2,1)S(1)}, u32[]{:S(2)}) copy-start(bf16[1,12,16,2048]{3,2,1,0:T(8,128)(2,1)S(1)} %get-tuple-element.258) | copy-start | bytes 2359300
where the time goes:
time: 78.4 us; the launch traced here: 77.8 us
  starting transfers between devices  55 us (70%)
  waiting for transfers between devices  13.2 us (17%)
  Pallas kernels  5.85 us (7%)
  between operations  1.98 us (3%)
  local copies, waits for them, and re-layouts  0.89 us (1%)
  loops' own time  0.86 us (1%)
    ppermute x3, waiting for transfers between devices, body(): lax.ppermute(stack, 'col', [(i, i ^ 2 * k) for i in range(col_count)])  13 us
    ppermute x4, starting transfers between devices, body(): lax.ppermute(part, 'col', near_pairs)  11 us
    ppermute x3, starting transfers between devices, body(): lax.ppermute(stack, 'col', [(i, i ^ 2 * k) for i in range(col_count)])  9.58 us
    ppermute x3, starting transfers between devices, body(): lax.ppermute(sent, 'row', [(i, i ^ k) for i in range(row_count)])  9.27 us
    ppermute x1, starting transfers between devices, body(): near = lax.ppermute(near, 'col', near_pairs)  7.1 us
    ppermute x1, starting transfers between devices, body(): answered = lax.ppermute(answer(asked, table, gate_weight), 'dp', ahead)  4.04 us
    ppermute x1, starting transfers between devices, body(): far = lax.ppermute(far, 'col', far_pairs)  3.25 us
    ppermute x1, starting transfers between devices, body(): peer = lax.ppermute(out_weight, 'dp', ahead)  3.12 us
  transfers between devices with their start and end apart: 17, of which 3 were waited for; matrix products, arithmetic and copies ran while one was open for 0% of the time, Pallas kernels for 6%

commit v1 on v0

--- a/solution.py
+++ b/solution.py
@@ -17,7 +17,7 @@
 PAD_ROWS = 2
 
 
-def attend_kernel(q_ref, kv_ref, up_ref, down_ref, near_ref, far_ref, out_ref):
+def attend_kernel(q_ref, kv_ref, up_ref, down_ref, far_ref, near_ref, out_ref):
     rows, cols = 12, 16
     inner = q_ref.shape[1]
     row0 = lax.axis_index("row") * rows
@@ -79,7 +79,7 @@
             ).astype(BF16)
 
 
-def attend(q, kv, up, down, near, far):
+def attend(q, kv, up, down, far, near):
     tokens, inner = q.shape
     return pl.pallas_call(
         attend_kernel,
@@ -89,7 +89,7 @@
         compiler_params=pltpu.CompilerParams(vmem_limit_bytes=20 * 2**20),
         cost_estimate=pl.CostEstimate(flops=3000000000, bytes_accessed=0, transcendentals=0),
         name="attend",
-    )(q, kv, up, down, near, far)
+    )(q, kv, up, down, far, near)
 
 
 def in_vmem(count):
@@ -436,7 +436,7 @@
         near, far = edges(kv, up, down, sent)
         far = lax.ppermute(far, "col", far_pairs)
         near = lax.ppermute(near, "col", near_pairs)
-        attended = attend(q, kv, up, down, near, far)
+        attended = attend(q, kv, up, down, far, near)
         mine, attended = lax.optimization_barrier((stack, attended))
         siblings = [lax.ppermute(part, "col", near_pairs) for part in (mine, opposite, other, beside)]
         mine_x, opposite_x, other_x, beside_x = siblings

time: 78.4 us -> 96.8 us (1.23)
  the two profiles are of different devices: /device:TPU:293 before, /device:TPU:1 now
where the time goes in v1:
time: 96.8 us; the launch traced here: 96.1 us
  starting transfers between devices  69.3 us (72%)
  waiting for transfers between devices  17.5 us (18%)
  Pallas kernels  5.84 us (6%)
  between operations  1.98 us (2%)
    ppermute x1, starting transfers between devices, body(): asked = lax.ppermute(ask, 'dp', behind)  15.5 us
    ppermute x4, starting transfers between devices, body(): lax.ppermute(part, 'col', near_pairs)  13.6 us
    ppermute x3, starting transfers between devices, body(): lax.ppermute(sent, 'row', [(i, i ^ k) for i in range(row_count)])  12.8 us
    ppermute x3, waiting for transfers between devices, body(): lax.ppermute(stack, 'col', [(i, i ^ 2 * k) for i in range(col_count)])  10.4 us
    ppermute x3, starting transfers between devices, body(): lax.ppermute(stack, 'col', [(i, i ^ 2 * k) for i in range(col_count)])  9.58 us
    ppermute x1, starting transfers between devices, body(): far = lax.ppermute(far, 'col', far_pairs)  6.94 us
    ppermute x1, waiting for transfers between devices, body(): answered = lax.ppermute(answer(asked, table, gate_weight), 'dp', ahead)  6.86 us
    ppermute x1, starting transfers between devices, body(): answered = lax.ppermute(answer(asked, table, gate_weight), 'dp', ahead)  2.98 us
  transfers between devices with their start and end apart: 17, of which 4 were waited for; matrix products, arithmetic and copies ran while one was open for 0% of the time, Pallas kernels for 5%

profile of v1, /device:TPU:1, one launch (start us, length us, event | category | flops | bytes accessed | tf_op | source)
XLA Modules:
  0.0 96.1 jit_solution(3473709966079115324)
XLA Ops:
  2.0 1.1 %begin.1 = (f32[1,256]{1,0:T(1,128)S(1)}, bf16[64,1000]{1,0:T(8,128)(2,1)S(1)}, bf16[64,2048]{1,0:T(8,128)(2,1)S(1)}) custom-call(s32[1]{0:T(128)S(6)} %copy.17.label_ref, s32[1]{0:T(128)S(6)} %copy.18.step_ref, bf16[64,1000]{1,0:T(8,128)(2,1)} %bitcast.24, bf16[64,2048]{1,0:T(8,128)(2,1)} %bitcast.23), custom_call_target="tpu_custom_call" | custom-call | tf_op jit(solution)/shard_map/begin/pallas_call | solution.py:167
  3.1 92.2 %conditional.1 = (bf16[1,12,16,2048]{3,2,1,0:T(8,128)(2,1)S(1)}) conditional(s32[]{:T(128)} %clamp.3, (bf16[32,2048]{1,0:T(8,128)(2,1)}, f32[1,256]{1,0:T(1,128)S(1)}, bf16[64,1000]{1,0:T(8,128)(2,1)S(1)}, bf16[64,2048]{1,0:T(8,128)(2,1)S(1)}, bf16[2,192,1024]{2,1,0:T(8,128)(2,1)}, ...), branch_computations={%region_0.1_spmd, %region_1.2_spmd, %region_2.3_spmd, %region_3.4_... | conditional | flops 17999998976 | bytes 27300612 | solution.py:448
  3.1 15.5 %collective-permute-start.1 = (f32[1,256]{1,0:T(1,128)S(1)}, f32[1,256]{1,0:T(1,128)S(1)}, u32[]{:S(2)}, u32[]{:S(2)}) collective-permute-start(f32[1,256]{1,0:T(1,128)S(1)} %get-tuple-element.60.ask_ref.after_ref), channel_id=1, source_target_pairs={{32,0},{64,32},{96,64},{128,96},{160,128},{192,160},{224,192},{256... | collective-permute-start | bytes 3080 | tf_op jit(solution)/shard_map/cond/branch_0_fun/ppermute | solution.py:422
  18.6 1.9 %collective-permute-start = (bf16[32,2048]{1,0:T(8,128)(2,1)}, bf16[32,2048]{1,0:T(8,128)(2,1)S(1)}, u32[]{:S(2)}, u32[]{:S(2)}) collective-permute-start(bf16[32,2048]{1,0:T(8,128)(2,1)} %get-tuple-element.58.own_ref), channel_id=1, source_target_pairs={{0,32},{32,64},{64,96},{96,128},{128,160},{160,192},{192,224},{224... | collective-permute-start | bytes 393224 | tf_op jit(solution)/shard_map/cond/branch_0_fun/ppermute | solution.py:423
  20.5 0.0 collective-permute-done.1.asked_ref
  20.5 0.0 copy-start
  20.5 0.0 copy-start.9
  20.5 0.4 answer.4
  20.9 3.0 %collective-permute-start.2 = (bf16[32,256]{1,0:T(8,128)(2,1)S(1)}, bf16[32,256]{1,0:T(8,128)(2,1)S(1)}, u32[]{:S(2)}, u32[]{:S(2)}) collective-permute-start(bf16[32,256]{1,0:T(8,128)(2,1)S(1)} %answer.4), channel_id=1, source_target_pairs={{0,32},{32,64},{64,96},{96,128},{128,160},{160,192},{192,224},{224... | collective-permute-start | bytes 49160 | tf_op jit(solution)/shard_map/cond/branch_0_fun/ppermute | solution.py:427
  23.9 0.3 cut.4
  24.2 2.7 %collective-permute-start.6 = (bf16[2,48,1024]{2,1,0:T(8,128)(2,1)S(1)}, bf16[2,48,1024]{2,1,0:T(8,128)(2,1)S(1)}, u32[]{:S(2)}, u32[]{:S(2)}) collective-permute-start(bf16[2,48,1024]{2,1,0:T(8,128)(2,1)S(1)} %get-tuple-element.65), channel_id=1, source_target_pairs={{0,8},{8,16},{16,24},{1,9},{9,17},{17,25},{2,10},{10,18},{18,26},{... | collective-permute-start | bytes 589832 | tf_op jit(solution)/shard_map/cond/branch_0_fun/ppermute | solution.py:425
  26.9 1.3 %collective-permute-start.7 = (bf16[2,48,1024]{2,1,0:T(8,128)(2,1)S(1)}, bf16[2,48,1024]{2,1,0:T(8,128)(2,1)S(1)}, u32[]{:S(2)}, u32[]{:S(2)}) collective-permute-start(bf16[2,48,1024]{2,1,0:T(8,128)(2,1)S(1)} %get-tuple-element.66), channel_id=1, source_target_pairs={{8,0},{16,8},{24,16},{9,1},{17,9},{25,17},{10,2},{18,10},{26,18},{... | collective-permute-start | bytes 589832 | tf_op jit(solution)/shard_map/cond/branch_0_fun/ppermute | solution.py:426
  28.2 6.9 %collective-permute-done.2.answered_ref = bf16[32,256]{1,0:T(8,128)(2,1)S(1)} collective-permute-done((bf16[32,256]{1,0:T(8,128)(2,1)S(1)}, bf16[32,256]{1,0:T(8,128)(2,1)S(1)}, u32[]{:S(2)}, u32[]{:S(2)}) %collective-permute-start.2) | collective-permute-done | bytes 16416 | tf_op jit(solution)/shard_map/cond/branch_0_fun/ppermute | solution.py:427
  35.0 0.0 collective-permute-done.peer_ref
  35.1 0.2 mix.4.refs_0_.after_ref
  35.3 6.6 %collective-permute-start.3 = (bf16[32,2176]{1,0:T(8,128)(2,1)S(1)}, bf16[32,2176]{1,0:T(8,128)(2,1)S(1)}, u32[]{:S(2)}, u32[]{:S(2)}) collective-permute-start(bf16[32,2176]{1,0:T(8,128)(2,1)S(1)} %mix.4.refs_0_.after_ref), channel_id=1, source_target_pairs={{0,16},{8,24},{16,0},{24,8},{1,17},{9,25},{17,1},{25,9},{2,18},{10... | collective-permute-start | bytes 417800 | tf_op jit(solution)/shard_map/cond/branch_0_fun/ppermute | solution.py:430
  41.9 4.0 %collective-permute-start.4 = (bf16[32,2176]{1,0:T(8,128)(2,1)S(1)}, bf16[32,2176]{1,0:T(8,128)(2,1)S(1)}, u32[]{:S(2)}, u32[]{:S(2)}) collective-permute-start(bf16[32,2176]{1,0:T(8,128)(2,1)S(1)} %mix.4.refs_0_.after_ref), channel_id=1, source_target_pairs={{0,24},{8,16},{16,8},{24,0},{1,25},{9,17},{17,9},{25,1},{2,26},{10... | collective-permute-start | bytes 417800 | tf_op jit(solution)/shard_map/cond/branch_0_fun/ppermute | solution.py:430
  45.9 2.2 %collective-permute-start.5 = (bf16[32,2176]{1,0:T(8,128)(2,1)S(1)}, bf16[32,2176]{1,0:T(8,128)(2,1)S(1)}, u32[]{:S(2)}, u32[]{:S(2)}) collective-permute-start(bf16[32,2176]{1,0:T(8,128)(2,1)S(1)} %mix.4.refs_0_.after_ref), channel_id=1, source_target_pairs={{0,8},{8,0},{16,24},{24,16},{1,9},{9,1},{17,25},{25,17},{2,10},{10... | collective-permute-start | bytes 417800 | tf_op jit(solution)/shard_map/cond/branch_0_fun/ppermute | solution.py:430
  48.1 0.0 collective-permute-done.6.up_ref
  48.1 0.0 collective-permute-done.7.down_ref
  48.2 0.7 edges.4
  48.8 6.9 %collective-permute-start.8 = (bf16[2,80,1024]{2,1,0:T(8,128)(2,1)S(1)}, bf16[2,80,1024]{2,1,0:T(8,128)(2,1)S(1)}, u32[]{:S(2)}, u32[]{:S(2)}) collective-permute-start(bf16[2,80,1024]{2,1,0:T(8,128)(2,1)S(1)} %get-tuple-element.67), channel_id=1, source_target_pairs={{1,2},{3,4},{5,6},{2,1},{4,3},{6,5},{9,10},{11,12},{13,14},{10,9},... | collective-permute-start | bytes 983048 | tf_op jit(solution)/shard_map/cond/branch_0_fun/ppermute | solution.py:437
  55.8 0.0 copy-start.5
  55.8 2.1 %collective-permute-start.9 = (bf16[2,80,1024]{2,1,0:T(8,128)(2,1)S(1)}, bf16[2,80,1024]{2,1,0:T(8,128)(2,1)S(1)}, u32[]{:S(2)}, u32[]{:S(2)}) collective-permute-start(bf16[2,80,1024]{2,1,0:T(8,128)(2,1)S(1)} %get-tuple-element.68), channel_id=1, source_target_pairs={{0,1},{1,0},{2,3},{3,2},{4,5},{5,4},{6,7},{7,6},{8,9},{9,8},{10,11... | collective-permute-start | bytes 983048 | tf_op jit(solution)/shard_map/cond/branch_0_fun/ppermute | solution.py:438
  57.9 0.0 collective-permute-done.3.refs_1_
  57.9 0.0 collective-permute-done.4.refs_2_
  57.9 0.0 collective-permute-done.5.refs_3_
  57.9 3.5 %collective-permute-start.10 = (bf16[128,2176]{1,0:T(8,128)(2,1)S(1)}, bf16[128,2176]{1,0:T(8,128)(2,1)S(1)}, u32[]{:S(2)}, u32[]{:S(2)}) collective-permute-start(bf16[128,2176]{1,0:T(8,128)(2,1)S(1)} %stack.4.own), channel_id=1, source_target_pairs={{0,6},{1,7},{2,4},{3,5},{4,2},{5,3},{6,0},{7,1},{8,14},{9,15},{10,... | collective-permute-start | bytes 1671176 | tf_op jit(solution)/shard_map/cond/branch_0_fun/ppermute | solution.py:434
  61.4 2.7 %collective-permute-start.11 = (bf16[128,2176]{1,0:T(8,128)(2,1)S(1)}, bf16[128,2176]{1,0:T(8,128)(2,1)S(1)}, u32[]{:S(2)}, u32[]{:S(2)}) collective-permute-start(bf16[128,2176]{1,0:T(8,128)(2,1)S(1)} %stack.4.own), channel_id=1, source_target_pairs={{0,2},{1,3},{2,0},{3,1},{4,6},{5,7},{6,4},{7,5},{8,10},{9,11},{10,... | collective-permute-start | bytes 1671176 | tf_op jit(solution)/shard_map/cond/branch_0_fun/ppermute | solution.py:434
  64.1 3.5 %collective-permute-start.15 = (bf16[128,2176]{1,0:T(8,128)(2,1)S(1)}, bf16[128,2176]{1,0:T(8,128)(2,1)S(1)}, u32[]{:S(2)}, u32[]{:S(2)}) collective-permute-start(bf16[128,2176]{1,0:T(8,128)(2,1)S(1)} %stack.4.own), channel_id=1, source_target_pairs={{0,4},{1,5},{2,6},{3,7},{4,0},{5,1},{6,2},{7,3},{8,12},{9,13},{10,... | collective-permute-start | bytes 1671176 | tf_op jit(solution)/shard_map/cond/branch_0_fun/ppermute | solution.py:434
  67.6 0.0 collective-permute-done.8.far_ref
  67.6 0.0 collective-permute-done.9.near_ref
  67.6 1.4 %attend.4.a_ref = bf16[192,1024]{1,0:T(8,128)(2,1)S(1)} custom-call(bf16[192,1024]{1,0:T(8,128)(2,1)S(1)} %copy-done.5, bf16[2,192,1024]{2,1,0:T(8,128)(2,1)S(1)} %copy-done, bf16[2,48,1024]{2,1,0:T(8,128)(2,1)S(1)} %collective-permute-done.6.up_ref, bf16[2,48,1024]{2,1,0:T(8,128)(2,1)S(1)} %collective-permute-done.7.down_ref, ...), custom_call_target="tpu_custom_call" | custom-call | flops 3000000000 | tf_op jit(solution)/shard_map/cond/branch_0_fun/attend/pallas_call | solution.py:84
  69.0 3.2 %collective-permute-start.12 = (bf16[128,2176]{1,0:T(8,128)(2,1)S(1)}, bf16[128,2176]{1,0:T(8,128)(2,1)S(1)}, u32[]{:S(2)}, u32[]{:S(2)}) collective-permute-start(bf16[128,2176]{1,0:T(8,128)(2,1)S(1)} %stack.4.own), channel_id=1, source_target_pairs={{0,1},{1,0},{2,3},{3,2},{4,5},{5,4},{6,7},{7,6},{8,9},{9,8},{10,11... | collective-permute-start | bytes 1671176 | tf_op jit(solution)/shard_map/cond/branch_0_fun/ppermute | solution.py:441
  72.2 2.5 %collective-permute-done.10.other = bf16[128,2176]{1,0:T(8,128)(2,1)S(1)} collective-permute-done((bf16[128,2176]{1,0:T(8,128)(2,1)S(1)}, bf16[128,2176]{1,0:T(8,128)(2,1)S(1)}, u32[]{:S(2)}, u32[]{:S(2)}) %collective-permute-start.10) | collective-permute-done | bytes 557088 | tf_op jit(solution)/shard_map/cond/branch_0_fun/ppermute | solution.py:434
  74.7 3.2 %collective-permute-start.13 = (bf16[128,2176]{1,0:T(8,128)(2,1)S(1)}, bf16[128,2176]{1,0:T(8,128)(2,1)S(1)}, u32[]{:S(2)}, u32[]{:S(2)}) collective-permute-start(bf16[128,2176]{1,0:T(8,128)(2,1)S(1)} %collective-permute-done.10.other), channel_id=1, source_target_pairs={{0,1},{1,0},{2,3},{3,2},{4,5},{5,4},{6,7},{7,6},{8,9},{9,8},{10,11... | collective-permute-start | bytes 1671176 | tf_op jit(solution)/shard_map/cond/branch_0_fun/ppermute | solution.py:441
  78.0 0.0 collective-permute-done.11.beside
  78.0 3.5 %collective-permute-start.14 = (bf16[128,2176]{1,0:T(8,128)(2,1)S(1)}, bf16[128,2176]{1,0:T(8,128)(2,1)S(1)}, u32[]{:S(2)}, u32[]{:S(2)}) collective-permute-start(bf16[128,2176]{1,0:T(8,128)(2,1)S(1)} %collective-permute-done.11.beside), channel_id=1, source_target_pairs={{0,1},{1,0},{2,3},{3,2},{4,5},{5,4},{6,7},{7,6},{8,9},{9,8},{10,11... | collective-permute-start | bytes 1671176 | tf_op jit(solution)/shard_map/cond/branch_0_fun/ppermute | solution.py:441
  81.5 7.9 %collective-permute-done.15.piece = bf16[128,2176]{1,0:T(8,128)(2,1)S(1)} collective-permute-done((bf16[128,2176]{1,0:T(8,128)(2,1)S(1)}, bf16[128,2176]{1,0:T(8,128)(2,1)S(1)}, u32[]{:S(2)}, u32[]{:S(2)}) %collective-permute-start.15) | collective-permute-done | bytes 557088 | tf_op jit(solution)/shard_map/cond/branch_0_fun/ppermute | solution.py:434
  89.5 3.6 %collective-permute-start.16 = (bf16[128,2176]{1,0:T(8,128)(2,1)S(1)}, bf16[128,2176]{1,0:T(8,128)(2,1)S(1)}, u32[]{:S(2)}, u32[]{:S(2)}) collective-permute-start(bf16[128,2176]{1,0:T(8,128)(2,1)S(1)} %collective-permute-done.15.piece), channel_id=1, source_target_pairs={{0,1},{1,0},{2,3},{3,2},{4,5},{5,4},{6,7},{7,6},{8,9},{9,8},{10,11... | collective-permute-start | bytes 1671176 | tf_op jit(solution)/shard_map/cond/branch_0_fun/ppermute | solution.py:441
  93.0 0.0 collective-permute-done.12.own_x
  93.0 0.0 collective-permute-done.13.other_x
  93.1 0.0 collective-permute-done.14.beside_x
  93.1 1.3 %begin_project.4 = (f32[192,2048]{1,0:T(8,128)S(1)}, bf16[192,256]{1,0:T(8,128)(2,1)S(1)}, f32[32,128]{1,0:T(8,128)S(1)}) custom-call(bf16[192,1024]{1,0:T(8,128)(2,1)S(1)} %attend.4.a_ref, bf16[128,2176]{1,0:T(8,128)(2,1)S(1)} %stack.4.own, bf16[128,2176]{1,0:T(8,128)(2,1)S(1)} %collective-permute-done.10.other, ...), custom_call_target="tpu_custom_call" | custom-call | tf_op jit(solution)/shard_map/cond/branch_0_fun/begin_project/pallas_call | solution.py:358
  94.4 0.2 collective-permute-done.16.piece_x
  94.6 0.4 project.4
  95.3 0.0 copy-start.4
  95.3 0.9 copy-done.4
  (4 shorter events, 0.0 us)
Async XLA Ops:
  3.1 17.4 %collective-permute-start.1 = (f32[1,256]{1,0:T(1,128)S(1)}, f32[1,256]{1,0:T(1,128)S(1)}, u32[]{:S(2)}, u32[]{:S(2)}) collective-permute-start(f32[1,256]{1,0:T(1,128)S(1)} %get-tuple-element.60.ask_ref.after_ref), channel_id=1, source_target_pairs={{32,0},{64,32},{96,64},{128,96},{160,128},{192,160},{224,192},{256... | collective-permute-start | bytes 3080 | tf_op jit(solution)/shard_map/cond/branch_0_fun/ppermute | solution.py:422
  18.6 16.5 %collective-permute-start = (bf16[32,2048]{1,0:T(8,128)(2,1)}, bf16[32,2048]{1,0:T(8,128)(2,1)S(1)}, u32[]{:S(2)}, u32[]{:S(2)}) collective-permute-start(bf16[32,2048]{1,0:T(8,128)(2,1)} %get-tuple-element.58.own_ref), channel_id=1, source_target_pairs={{0,32},{32,64},{64,96},{96,128},{128,160},{160,192},{192,224},{224... | collective-permute-start | bytes 393224 | tf_op jit(solution)/shard_map/cond/branch_0_fun/ppermute | solution.py:423
  20.5 3.4 %copy-start = (bf16[2,192,1024]{2,1,0:T(8,128)(2,1)S(1)}, bf16[2,192,1024]{2,1,0:T(8,128)(2,1)}, u32[]{:S(2)}) copy-start(bf16[2,192,1024]{2,1,0:T(8,128)(2,1)} %get-tuple-element.64.kv_ref) | copy-start | bytes 2359300 | tf_op jit(solution)/shard_map/cond
  20.5 14.5 %copy-start.9 = (bf16[32,2048]{1,0:T(8,128)(2,1)S(1)}, bf16[32,2048]{1,0:T(8,128)(2,1)}, u32[]{:S(2)}) copy-start(bf16[32,2048]{1,0:T(8,128)(2,1)} %get-tuple-element.58.own_ref) | copy-start | bytes 393220 | tf_op jit(solution)/shard_map/cond
  20.9 14.1 %collective-permute-start.2 = (bf16[32,256]{1,0:T(8,128)(2,1)S(1)}, bf16[32,256]{1,0:T(8,128)(2,1)S(1)}, u32[]{:S(2)}, u32[]{:S(2)}) collective-permute-start(bf16[32,256]{1,0:T(8,128)(2,1)S(1)} %answer.4), channel_id=1, source_target_pairs={{0,32},{32,64},{64,96},{96,128},{128,160},{160,192},{192,224},{224... | collective-permute-start | bytes 49160 | tf_op jit(solution)/shard_map/cond/branch_0_fun/ppermute | solution.py:427
  24.2 23.9 %collective-permute-start.6 = (bf16[2,48,1024]{2,1,0:T(8,128)(2,1)S(1)}, bf16[2,48,1024]{2,1,0:T(8,128)(2,1)S(1)}, u32[]{:S(2)}, u32[]{:S(2)}) collective-permute-start(bf16[2,48,1024]{2,1,0:T(8,128)(2,1)S(1)} %get-tuple-element.65), channel_id=1, source_target_pairs={{0,8},{8,16},{16,24},{1,9},{9,17},{17,25},{2,10},{10,18},{18,26},{... | collective-permute-start | bytes 589832 | tf_op jit(solution)/shard_map/cond/branch_0_fun/ppermute | solution.py:425
  26.9 21.3 %collective-permute-start.7 = (bf16[2,48,1024]{2,1,0:T(8,128)(2,1)S(1)}, bf16[2,48,1024]{2,1,0:T(8,128)(2,1)S(1)}, u32[]{:S(2)}, u32[]{:S(2)}) collective-permute-start(bf16[2,48,1024]{2,1,0:T(8,128)(2,1)S(1)} %get-tuple-element.66), channel_id=1, source_target_pairs={{8,0},{16,8},{24,16},{9,1},{17,9},{25,17},{10,2},{18,10},{26,18},{... | collective-permute-start | bytes 589832 | tf_op jit(solution)/shard_map/cond/branch_0_fun/ppermute | solution.py:426
  35.3 22.6 %collective-permute-start.3 = (bf16[32,2176]{1,0:T(8,128)(2,1)S(1)}, bf16[32,2176]{1,0:T(8,128)(2,1)S(1)}, u32[]{:S(2)}, u32[]{:S(2)}) collective-permute-start(bf16[32,2176]{1,0:T(8,128)(2,1)S(1)} %mix.4.refs_0_.after_ref), channel_id=1, source_target_pairs={{0,16},{8,24},{16,0},{24,8},{1,17},{9,25},{17,1},{25,9},{2,18},{10... | collective-permute-start | bytes 417800 | tf_op jit(solution)/shard_map/cond/branch_0_fun/ppermute | solution.py:430
  41.9 15.9 %collective-permute-start.4 = (bf16[32,2176]{1,0:T(8,128)(2,1)S(1)}, bf16[32,2176]{1,0:T(8,128)(2,1)S(1)}, u32[]{:S(2)}, u32[]{:S(2)}) collective-permute-start(bf16[32,2176]{1,0:T(8,128)(2,1)S(1)} %mix.4.refs_0_.after_ref), channel_id=1, source_target_pairs={{0,24},{8,16},{16,8},{24,0},{1,25},{9,17},{17,9},{25,1},{2,26},{10... | collective-permute-start | bytes 417800 | tf_op jit(solution)/shard_map/cond/branch_0_fun/ppermute | solution.py:430
  45.9 12.0 %collective-permute-start.5 = (bf16[32,2176]{1,0:T(8,128)(2,1)S(1)}, bf16[32,2176]{1,0:T(8,128)(2,1)S(1)}, u32[]{:S(2)}, u32[]{:S(2)}) collective-permute-start(bf16[32,2176]{1,0:T(8,128)(2,1)S(1)} %mix.4.refs_0_.after_ref), channel_id=1, source_target_pairs={{0,8},{8,0},{16,24},{24,16},{1,9},{9,1},{17,25},{25,17},{2,10},{10... | collective-permute-start | bytes 417800 | tf_op jit(solution)/shard_map/cond/branch_0_fun/ppermute | solution.py:430
  48.8 18.7 %collective-permute-start.8 = (bf16[2,80,1024]{2,1,0:T(8,128)(2,1)S(1)}, bf16[2,80,1024]{2,1,0:T(8,128)(2,1)S(1)}, u32[]{:S(2)}, u32[]{:S(2)}) collective-permute-start(bf16[2,80,1024]{2,1,0:T(8,128)(2,1)S(1)} %get-tuple-element.67), channel_id=1, source_target_pairs={{1,2},{3,4},{5,6},{2,1},{4,3},{6,5},{9,10},{11,12},{13,14},{10,9},... | collective-permute-start | bytes 983048 | tf_op jit(solution)/shard_map/cond/branch_0_fun/ppermute | solution.py:437
  55.8 11.8 %copy-start.5 = (bf16[192,1024]{1,0:T(8,128)(2,1)S(1)}, bf16[192,1024]{1,0:T(8,128)(2,1)}, u32[]{:S(2)}) copy-start(bf16[192,1024]{1,0:T(8,128)(2,1)} %get-tuple-element.63.q_ref) | copy-start | bytes 1179652 | tf_op jit(solution)/shard_map/cond
  55.8 11.8 %collective-permute-start.9 = (bf16[2,80,1024]{2,1,0:T(8,128)(2,1)S(1)}, bf16[2,80,1024]{2,1,0:T(8,128)(2,1)S(1)}, u32[]{:S(2)}, u32[]{:S(2)}) collective-permute-start(bf16[2,80,1024]{2,1,0:T(8,128)(2,1)S(1)} %get-tuple-element.68), channel_id=1, source_target_pairs={{0,1},{1,0},{2,3},{3,2},{4,5},{5,4},{6,7},{7,6},{8,9},{9,8},{10,11... | collective-permute-start | bytes 983048 | tf_op jit(solution)/shard_map/cond/branch_0_fun/ppermute | solution.py:438
  57.9 16.8 %collective-permute-start.10 = (bf16[128,2176]{1,0:T(8,128)(2,1)S(1)}, bf16[128,2176]{1,0:T(8,128)(2,1)S(1)}, u32[]{:S(2)}, u32[]{:S(2)}) collective-permute-start(bf16[128,2176]{1,0:T(8,128)(2,1)S(1)} %stack.4.own), channel_id=1, source_target_pairs={{0,6},{1,7},{2,4},{3,5},{4,2},{5,3},{6,0},{7,1},{8,14},{9,15},{10,... | collective-permute-start | bytes 1671176 | tf_op jit(solution)/shard_map/cond/branch_0_fun/ppermute | solution.py:434
  61.4 16.6 %collective-permute-start.11 = (bf16[128,2176]{1,0:T(8,128)(2,1)S(1)}, bf16[128,2176]{1,0:T(8,128)(2,1)S(1)}, u32[]{:S(2)}, u32[]{:S(2)}) collective-permute-start(bf16[128,2176]{1,0:T(8,128)(2,1)S(1)} %stack.4.own), channel_id=1, source_target_pairs={{0,2},{1,3},{2,0},{3,1},{4,6},{5,7},{6,4},{7,5},{8,10},{9,11},{10,... | collective-permute-start | bytes 1671176 | tf_op jit(solution)/shard_map/cond/branch_0_fun/ppermute | solution.py:434
  64.1 25.4 %collective-permute-start.15 = (bf16[128,2176]{1,0:T(8,128)(2,1)S(1)}, bf16[128,2176]{1,0:T(8,128)(2,1)S(1)}, u32[]{:S(2)}, u32[]{:S(2)}) collective-permute-start(bf16[128,2176]{1,0:T(8,128)(2,1)S(1)} %stack.4.own), channel_id=1, source_target_pairs={{0,4},{1,5},{2,6},{3,7},{4,0},{5,1},{6,2},{7,3},{8,12},{9,13},{10,... | collective-permute-start | bytes 1671176 | tf_op jit(solution)/shard_map/cond/branch_0_fun/ppermute | solution.py:434
  69.0 24.0 %collective-permute-start.12 = (bf16[128,2176]{1,0:T(8,128)(2,1)S(1)}, bf16[128,2176]{1,0:T(8,128)(2,1)S(1)}, u32[]{:S(2)}, u32[]{:S(2)}) collective-permute-start(bf16[128,2176]{1,0:T(8,128)(2,1)S(1)} %stack.4.own), channel_id=1, source_target_pairs={{0,1},{1,0},{2,3},{3,2},{4,5},{5,4},{6,7},{7,6},{8,9},{9,8},{10,11... | collective-permute-start | bytes 1671176 | tf_op jit(solution)/shard_map/cond/branch_0_fun/ppermute | solution.py:441
  74.7 18.3 %collective-permute-start.13 = (bf16[128,2176]{1,0:T(8,128)(2,1)S(1)}, bf16[128,2176]{1,0:T(8,128)(2,1)S(1)}, u32[]{:S(2)}, u32[]{:S(2)}) collective-permute-start(bf16[128,2176]{1,0:T(8,128)(2,1)S(1)} %collective-permute-done.10.other), channel_id=1, source_target_pairs={{0,1},{1,0},{2,3},{3,2},{4,5},{5,4},{6,7},{7,6},{8,9},{9,8},{10,11... | collective-permute-start | bytes 1671176 | tf_op jit(solution)/shard_map/cond/branch_0_fun/ppermute | solution.py:441
  78.0 15.0 %collective-permute-start.14 = (bf16[128,2176]{1,0:T(8,128)(2,1)S(1)}, bf16[128,2176]{1,0:T(8,128)(2,1)S(1)}, u32[]{:S(2)}, u32[]{:S(2)}) collective-permute-start(bf16[128,2176]{1,0:T(8,128)(2,1)S(1)} %collective-permute-done.11.beside), channel_id=1, source_target_pairs={{0,1},{1,0},{2,3},{3,2},{4,5},{5,4},{6,7},{7,6},{8,9},{9,8},{10,11... | collective-permute-start | bytes 1671176 | tf_op jit(solution)/shard_map/cond/branch_0_fun/ppermute | solution.py:441
  89.5 5.1 %collective-permute-start.16 = (bf16[128,2176]{1,0:T(8,128)(2,1)S(1)}, bf16[128,2176]{1,0:T(8,128)(2,1)S(1)}, u32[]{:S(2)}, u32[]{:S(2)}) collective-permute-start(bf16[128,2176]{1,0:T(8,128)(2,1)S(1)} %collective-permute-done.15.piece), channel_id=1, source_target_pairs={{0,1},{1,0},{2,3},{3,2},{4,5},{5,4},{6,7},{7,6},{8,9},{9,8},{10,11... | collective-permute-start | bytes 1671176 | tf_op jit(solution)/shard_map/cond/branch_0_fun/ppermute | solution.py:441
  95.3 0.9 copy-start.4
